TPU v7x, 512 devices: a whole 4x8x8 slice. The times are simulated.
512 devices in a mesh: elem: 16 (over y, x_hi), pulse: 32 (over x_lo, z, core).
Axes of the slice: x: 4 (x_hi: 2, x_lo: 2; x = x_hi * 2 + x_lo), y: 8, z: 8, core: 2. Of those that a mesh axis runs over, the one named last changes fastest.
Arguments:
- echoes: bfloat16 [2, 2048, 256, 1024], P(None, 'elem', 'pulse'), may hold values from -6 to 6
- keep_mask: int32 [256, 32], P('pulse'), may hold values from 0 to 1, as said below
- steer_index: int32 [512], replicated, may hold values from 0 to 1023
- element_position: float32 [2048], replicated, may hold values from 0 to 1024
- element_gain: float32 [2, 2048], replicated, may hold values from -4 to 4
- steer_sines: float32 [1024], replicated, may hold values from -1 to 1
Outputs:
- doppler_power: float32 [512, 256, 1024], P('pulse', None, 'elem')
Inputs may be any that keep to these rules, and one draw needn't show every extreme that they name: `keep_mask`: in each masking block, each aligned run of 8 pulses keeps at most 6 pulses, and at least one; in every masking block some run keeps exactly 6.
All inputs are finite; a program needn't handle non-finite values.
Results may differ from a plain program's by a relative error of at most 0.005.
Values may be sent and summed in bfloat16 or wider, within the bound.
A program may use at most 128 MiB of HBM per device.

v0:
```python
import functools
import math

import jax
import jax.numpy as jnp
from jax import lax
from jax.experimental import pallas as pl
from jax.experimental.pallas import tpu as pltpu
from jax.sharding import PartitionSpec as P

F32 = jnp.float32
BF16 = jnp.bfloat16
I32 = jnp.int32
E = 2048
BEAMS = 512
PULSES = 256
CELLS = 1024
BLOCKS = 32
RUN = 8
SLOTS = 6
NE = 16
NP = 32
LE = E // NE
LB = BEAMS // NP
LC = CELLS // NE
CHUNKS = 3


def turn(t):
    a = t * math.pi
    q = a * a
    s = a * (1.0 + q * (-1 / 6 + q * (1 / 120 + q * (-1 / 5040 + q * (1 / 362880 - q / 39916800)))))
    c = 1.0 + q * (-1 / 2 + q * (1 / 24 + q * (-1 / 720 + q * (1 / 40320 + q * (-1 / 3628800 + q / 479001600)))))
    return 1.0 - 2.0 * s * s, 2.0 * s * c


def iota(shape, dim):
    return lax.broadcasted_iota(I32, shape, dim)


def slot_pulses(keep):
    count = jnp.zeros_like(keep[0:1])
    first = jnp.zeros_like(count)
    second = jnp.zeros_like(count)
    for p in range(RUN):
        count = count + (1.0 - keep[p : p + 1])
        first = first + jnp.where(count < 0.5, 1.0, 0.0)
        second = second + jnp.where(count < 1.5, 1.0, 0.0)
    return [
        s + jnp.where(first < s + 0.5, 1.0, 0.0) + jnp.where(second < s + 1.5, 1.0, 0.0)
        for s in range(SLOTS)
    ]


def kernel(
    x_ref, mask_ref, index_ref, pos_ref, gain_ref, sines_ref, out_ref,
    prep, xbuf, wr, wi, beams, ybuf, fbuf, mine, mbuf, coef, perm, tab, tsel, xt, column,
    msend, mrecv, xsend, xrecv, bsend, brecv,
):
    em = lax.axis_index("elem")
    pm = lax.axis_index("pulse")
    barrier = pltpu.get_barrier_semaphore()

    def elem_peer(k):
        return lax.rem(em + k, NE)

    def pulse_peer(k):
        return lax.rem(pm + k, NP)

    def greet_elem(k, carry):
        pl.semaphore_signal(barrier, inc=1, device_id=(elem_peer(k), pm), device_id_type=pl.DeviceIdType.MESH)
        return carry

    def greet_pulse(k, carry):
        pl.semaphore_signal(barrier, inc=1, device_id=(em, pulse_peer(k)), device_id_type=pl.DeviceIdType.MESH)
        return carry

    lax.fori_loop(1, NE, greet_elem, 0)
    lax.fori_loop(1, NP, greet_pulse, 0)

    keep = mask_ref[...].astype(F32)
    blocks_of = iota((BLOCKS, CELLS), 1) // (CELLS // BLOCKS) == iota((BLOCKS, CELLS), 0)
    keep_cells = jnp.dot(keep, jnp.where(blocks_of, 1.0, 0.0), preferred_element_type=F32)
    pulses = slot_pulses(keep_cells)
    for s in range(SLOTS):
        for d in range(3):
            use = jnp.where(jnp.abs(pulses[s] - (s + d)) < 0.5, 1.0, 0.0)
            coef[3 * s + d : 3 * s + d + 1, :] = use * keep_cells[s + d : s + d + 1]
    narrow = jnp.where(iota((BLOCKS, 128), 1) == iota((BLOCKS, 128), 0), 1.0, 0.0)
    pulses = slot_pulses(jnp.dot(keep, narrow, preferred_element_type=F32))
    mine[...] = jnp.zeros_like(mine)
    for s in range(SLOTS):
        mine[s : s + 1, :] = pulses[s]
    mbuf[pl.ds(pl.multiple_of(pm * RUN, RUN), RUN), :] = mine[...]

    row, col = iota((256, 256), 0), iota((256, 256), 1)
    hit = (row // 32 == col % 8) & (row % 32 == col // 8)
    perm[...] = jnp.where(hit, 1.0, 0.0).astype(BF16)

    low_half = iota((32, 128), 1) < LC

    def pack(step, carry):
        pair = step // 8
        c = (step // 4) % 2
        group = step % 4
        lanes = pl.ds(pl.multiple_of(pair * 256, 256), 256)
        rows = pl.ds(pl.multiple_of(group * 256, 256), 256)
        turned = jnp.dot(perm[...], x_ref[c, rows, lanes], preferred_element_type=F32)
        parts = [turned[32 * p : 32 * p + 32] for p in range(RUN)]
        slots = []
        for s in range(SLOTS):
            total = parts[s] * coef[3 * s : 3 * s + 1, lanes]
            for d in (1, 2):
                total = total + parts[s + d] * coef[3 * s + d : 3 * s + d + 1, lanes]
            slots.append(total)
        for t in range(2):
            for j in range(CHUNKS):
                a = slots[j][:, 128 * t : 128 * t + 128]
                b = slots[j + 3][:, 128 * t : 128 * t + 128]
                first = jnp.where(low_half, a, pltpu.roll(b, LC, 1))
                second = jnp.where(low_half, pltpu.roll(a, LC, 1), b)
                at = pl.ds(pl.multiple_of(group * 32, 32), 32)
                to = pl.ds(pl.multiple_of(c * 128, 128), 128)
                prep[j, 4 * pair + 2 * t, at, to] = first.astype(BF16)
                prep[j, 4 * pair + 2 * t + 1, at, to] = second.astype(BF16)
        return carry

    lax.fori_loop(0, 32, pack, 0)

    pl.semaphore_wait(barrier, NE + NP - 2)

    my_rows = pl.ds(pl.multiple_of(em * LE, LE), LE)

    def send_samples(j):
        def one(k, carry):
            pltpu.make_async_remote_copy(
                src_ref=prep.at[j, elem_peer(k)],
                dst_ref=xbuf.at[j, my_rows],
                send_sem=xsend.at[j],
                recv_sem=xrecv.at[j],
                device_id=(elem_peer(k), pm),
                device_id_type=pl.DeviceIdType.MESH,
            ).start()
            return carry

        lax.fori_loop(1, NE, one, 0)

    def send_slots(k, carry):
        pltpu.make_async_remote_copy(
            src_ref=mine,
            dst_ref=mbuf.at[pl.ds(pl.multiple_of(pm * RUN, RUN), RUN)],
            send_sem=msend,
            recv_sem=mrecv,
            device_id=(em, pulse_peer(k)),
            device_id_type=pl.DeviceIdType.MESH,
        ).start()
        return carry

    send_samples(0)
    lax.fori_loop(1, NP, send_slots, 0)
    send_samples(1)
    send_samples(2)
    for j in range(CHUNKS):
        xbuf[j, my_rows, :] = prep[j, em]

    eye = iota((128, 128), 0) == iota((128, 128), 1)
    for i in range(BEAMS // 128):
        line = index_ref[0:1, 128 * i : 128 * i + 128].astype(F32)
        wanted = jnp.sum(jnp.where(eye, line, 0.0), axis=1, keepdims=True)
        choice = iota((128, sines_ref.shape[1]), 1).astype(F32) == wanted
        picked = jnp.sum(jnp.where(choice, sines_ref[...], 0.0), axis=1, keepdims=True)
        column[128 * i : 128 * i + 128, :] = jnp.broadcast_to(picked, (128, 128))

    factor = 1.0 / math.sqrt(E)

    def weigh(step, carry):
        rows = pl.ds(pl.multiple_of((step // 16) * 64, 64), 64)
        lanes = pl.ds(pl.multiple_of((step % 16) * 128, 128), 128)
        turns = pos_ref[0:1, lanes] * column[rows, :]
        cosine, sine = turn(turns - jnp.round(turns))
        real, imag = gain_ref[0:1, lanes] * factor, gain_ref[1:2, lanes] * factor
        wr[rows, lanes] = (real * cosine + imag * sine).astype(BF16)
        wi[rows, lanes] = (imag * cosine - real * sine).astype(BF16)
        return carry

    lax.fori_loop(0, 8 * 16, weigh, 0)

    def tabulate(step, carry):
        rows = pl.ds(pl.multiple_of(step * 32, 32), 32)
        p = iota((32, PULSES), 0) + step * 32
        product = jnp.bitwise_and(p * iota((32, PULSES), 1), PULSES - 1).astype(F32) / PULSES
        cosine, sine = turn(jnp.where(product < 0.5, product, product - 1.0))
        at = p.astype(F32) / (PULSES - 1)
        level, _ = turn(jnp.where(at < 0.5, at, at - 1.0))
        taper = (0.54 - 0.46 * level) / math.sqrt(PULSES)
        for i, value in enumerate((cosine * taper, sine * taper)):
            high = value.astype(BF16)
            tab[rows, 256 * i : 256 * i + 256] = high
            tab[rows, 512 + 256 * i : 512 + 256 * i + 256] = (value - high.astype(F32)).astype(BF16)
        return carry

    lax.fori_loop(0, PULSES // 32, tabulate, 0)

    def wait_bytes(ref, sem):
        pltpu.make_async_copy(ref, ref, sem).wait()

    wait_bytes(mbuf.at[pl.ds(0, RUN * (NP - 1))], mrecv)
    lane = iota((128, 128), 1)
    for k in range(2):
        for h in range(2):
            found = [mbuf[pl.ds(j + 3 * h, NP, stride=RUN), :] for j in range(CHUNKS)]
            found = jnp.concatenate(found + [jnp.zeros((NP, 128), F32)], axis=0)
            pulse = jnp.sum(jnp.where(lane == 2 * em + k, found, 0.0), axis=1, keepdims=True)
            row = iota((128, PULSES), 0)
            target = (RUN * (row % NP)).astype(F32) + pulse
            hit = (jnp.abs(iota((128, PULSES), 1).astype(F32) - target) < 0.5) & (row < 96)
            rows = jnp.dot(jnp.where(hit, 1.0, 0.0).astype(BF16), tab[...], preferred_element_type=F32)
            for part in range(2):
                cosine = rows[:, 512 * part : 512 * part + 256]
                sine = rows[:, 512 * part + 256 : 512 * part + 512]
                real = slice(128 * h, 128 * h + 128)
                imag = slice(256 + 128 * h, 256 + 128 * h + 128)
                tsel[k, part, real, 0:256] = cosine.astype(BF16)
                tsel[k, part, real, 256:512] = (-sine).astype(BF16)
                tsel[k, part, imag, 0:256] = sine.astype(BF16)
                tsel[k, part, imag, 256:512] = cosine.astype(BF16)

    my_beams = pl.ds(pl.multiple_of(pm * LB, LB), LB)
    for j in range(CHUNKS):
        wait_bytes(xbuf.at[j, pl.ds(0, LE * (NE - 1))], xrecv.at[j])

        def form(m, carry, j=j):
            rows = pl.ds(pl.multiple_of(m * 256, 256), 256)
            by_real = jnp.dot(wr[rows, :], xbuf[j], preferred_element_type=F32)
            by_imag = jnp.dot(wi[rows, :], xbuf[j], preferred_element_type=F32)
            beams[j, rows, 0:128] = (by_real[:, 0:128] - by_imag[:, 128:256]).astype(BF16)
            beams[j, rows, 128:256] = (by_real[:, 128:256] + by_imag[:, 0:128]).astype(BF16)
            return carry

        lax.fori_loop(0, 2, form, 0)

        def send_beams(k, carry, j=j):
            pltpu.make_async_remote_copy(
                src_ref=beams.at[j, pl.ds(pl.multiple_of(pulse_peer(k) * LB, LB), LB)],
                dst_ref=ybuf.at[j, my_beams],
                send_sem=bsend.at[j],
                recv_sem=brecv.at[j],
                device_id=(em, pulse_peer(k)),
                device_id_type=pl.DeviceIdType.MESH,
            ).start()
            return carry

        lax.fori_loop(1, NP, send_beams, 0)
        ybuf[j, my_beams, :] = beams[j, my_beams, :]

    for j in range(CHUNKS):
        wait_bytes(ybuf.at[j, pl.ds(0, LB * (NP - 1))], brecv.at[j])
        fbuf[0, 512 * j : 512 * j + 512, :] = ybuf[j, :, 0:128].astype(F32)
        fbuf[1, 512 * j : 512 * j + 512, :] = ybuf[j, :, 128:256].astype(F32)

    for b in range(LB):
        for c in range(2):
            got = [fbuf[c, pl.ds(512 * j + b, NP, stride=LB), :] for j in range(CHUNKS)]
            got = jnp.concatenate(got + [jnp.zeros((NP, 128), F32)], axis=0)
            flat = got.T.astype(BF16)
            for h in range(2):
                for k in range(2):
                    xt[k, 32 * b : 32 * b + 32, 256 * c + 128 * h : 256 * c + 128 * h + 128] = flat[
                        64 * h + 32 * k : 64 * h + 32 * k + 32
                    ]

    for k in range(2):
        for m in range(4):
            left = xt[k, 128 * m : 128 * m + 128, :]
            spec = jnp.dot(left, tsel[k, 0], preferred_element_type=F32)
            spec = spec + jnp.dot(left, tsel[k, 1], preferred_element_type=F32)
            power = spec[:, 0:256] * spec[:, 0:256] + spec[:, 256:512] * spec[:, 256:512]
            out_ref[4 * m : 4 * m + 4, 32 * k : 32 * k + 32, :] = power.reshape(4, 32, 256)

    wait_bytes(mbuf.at[pl.ds(0, RUN * (NP - 1))], msend)
    for j in range(CHUNKS):
        wait_bytes(xbuf.at[j, pl.ds(0, LE * (NE - 1))], xsend.at[j])
        wait_bytes(ybuf.at[j, pl.ds(0, LB * (NP - 1))], bsend.at[j])


def per_device(echoes, keep_mask, steer_index, element_position, element_gain, steer_sines):
    vmem = pl.BlockSpec(memory_space=pltpu.VMEM)
    dma = pltpu.SemaphoreType.DMA
    power = pl.pallas_call(
        kernel,
        out_shape=jax.ShapeDtypeStruct((LB, LC, PULSES), F32),
        in_specs=[vmem] * 6,
        out_specs=vmem,
        scratch_shapes=[
            pltpu.VMEM((CHUNKS, NE, LE, 256), BF16),
            pltpu.VMEM((CHUNKS, E, 256), BF16),
            pltpu.VMEM((BEAMS, E), BF16),
            pltpu.VMEM((BEAMS, E), BF16),
            pltpu.VMEM((CHUNKS, BEAMS, 256), BF16),
            pltpu.VMEM((CHUNKS, BEAMS, 256), BF16),
            pltpu.VMEM((2, CHUNKS * BEAMS, 128), F32),
            pltpu.VMEM((RUN, 128), F32),
            pltpu.VMEM((RUN * NP, 128), F32),
            pltpu.VMEM((3 * SLOTS, CELLS), F32),
            pltpu.VMEM((256, 256), BF16),
            pltpu.VMEM((PULSES, 1024), BF16),
            pltpu.VMEM((2, 2, 512, 512), BF16),
            pltpu.VMEM((2, 512, 512), BF16),
            pltpu.VMEM((BEAMS, 128), F32),
            dma, dma, dma((CHUNKS,)), dma((CHUNKS,)), dma((CHUNKS,)), dma((CHUNKS,)),
        ],
        compiler_params=pltpu.CompilerParams(
            collective_id=0, has_side_effects=True, vmem_limit_bytes=48 << 20
        ),
        name="integrate",
    )(
        echoes.reshape(2, LE * RUN, CELLS),
        keep_mask,
        steer_index.reshape(1, -1),
        element_position.reshape(1, -1),
        element_gain,
        steer_sines.reshape(1, -1),
    )
    return jnp.transpose(power, (0, 2, 1))


def solution(mesh):
    placed = (P(None, "elem", "pulse", None), P("pulse", None), P(), P(), P(), P())
    return jax.shard_map(
        per_device, mesh=mesh, in_specs=placed, out_specs=P("pulse", None, "elem"), check_vma=False
    )
```

profile of v0, /device:TPU:1, one launch (start us, length us, event | category | flops | bytes accessed | tf_op | source)
XLA Modules:
  0.0 108.9 jit_solution(6417395944612738209)
XLA Ops:
  0.0 0.0 copy-start
  0.0 2.2 %copy-done = bf16[2,128,8,1024]{3,2,1,0:T(8,128)(2,1)S(1)} copy-done((bf16[2,128,8,1024]{3,2,1,0:T(8,128)(2,1)S(1)}, bf16[2,128,8,1024]{3,2,1,0:T(8,128)(2,1)}, u32[]{:S(2)}) %copy-start) | copy-done | bytes 4194328
  2.2 0.0 copy-start.1
  2.2 0.7 copy-done.1
  2.9 0.0 copy-start.2
  2.9 0.7 copy-done.2
  3.6 0.0 copy-start.3
  3.6 0.7 copy-done.3
  4.3 0.0 copy-start.4
  4.3 0.7 copy-done.4
  5.0 0.0 copy-start.5
  5.0 0.7 copy-done.5
  5.7 102.3 %integrate.1 = f32[16,64,256]{2,1,0:T(8,128)S(1)} custom-call(bf16[2,1024,1024]{2,1,0:T(8,128)(2,1)S(1)} %bitcast.6, s32[8,32]{1,0:T(8,128)S(1)} %copy-done.3, s32[1,512]{1,0:T(1,128)S(1)} %bitcast.9, f32[1,2048]{1,0:T(1,128)S(1)} %bitcast.7, f32[2,2048]{1,0:T(2,128)S(1)} %copy-done.1, f32[1,1024]{1,0:T(1,128)S(1)} %bitcast.8), custom_call_target="tpu_custom_call" | custom-call | tf_op jit(solution)/shard_map/integrate/pallas_call | solution.py:289
  107.9 1.0 copy.8
Async XLA Ops:
  0.0 2.2 %copy-start = (bf16[2,128,8,1024]{3,2,1,0:T(8,128)(2,1)S(1)}, bf16[2,128,8,1024]{3,2,1,0:T(8,128)(2,1)}, u32[]{:S(2)}) copy-start(bf16[2,128,8,1024]{3,2,1,0:T(8,128)(2,1)} %param.6) | copy-start | bytes 12582916
  2.2 0.7 copy-start.1
  2.9 0.7 copy-start.2
  3.6 0.7 copy-start.3
  4.3 0.7 copy-start.4
  5.0 0.7 copy-start.5
where the time goes:
time: 110 us; the launch traced here: 109 us
  Pallas kernels  102 us (93%)
  local copies, waits for them, and re-layouts  6.63 us (6%)
    pallas_call x1, Pallas kernels, per_device(): pl.pallas_call(kernel, out_shape=jax.ShapeDtypeStruct((LB, LC, PULSES), F...  102 us
    unnamed x13, local copies, waits for them, and re-layouts  6.63 us

commit v1 on v0

--- a/solution.py
+++ b/solution.py
@@ -24,6 +24,8 @@
 LB = BEAMS // NP
 LC = CELLS // NE
 CHUNKS = 3
+NY = 8
+ORDER = (3, 5, 4, 2, 6, 1, 7, 0)
 
 
 def turn(t):
@@ -53,14 +55,35 @@
 
 
 def kernel(
-    x_ref, mask_ref, index_ref, pos_ref, gain_ref, sines_ref, out_ref,
-    prep, xbuf, wr, wi, beams, ybuf, fbuf, mine, mbuf, coef, perm, tab, tsel, xt, column,
-    msend, mrecv, xsend, xrecv, bsend, brecv,
+    x_hbm, mask_hbm, index_hbm, pos_hbm, gain_hbm, sines_hbm, out_ref,
+    x_ref, mask_ref, index_ref, pos_ref, gain_ref, sines_ref, prep, xbuf, wr, wi, beams, ybuf, fbuf, mine, mbuf, coef, perm, tab, tsel, xt, column,
+    lsem, ssem, msend, mrecv, xsend, xrecv, bsend, brecv,
 ):
     em = lax.axis_index("elem")
     pm = lax.axis_index("pulse")
     barrier = pltpu.get_barrier_semaphore()
 
+    small = [
+        pltpu.make_async_copy(a, b, ssem.at[i])
+        for i, (a, b) in enumerate((
+            (mask_hbm, mask_ref), (index_hbm, index_ref), (pos_hbm, pos_ref), (gain_hbm, gain_ref), (sines_hbm, sines_ref)
+        ))
+    ]
+    for copy in small:
+        copy.start()
+
+    def y_at(k):
+        return lax.rem(em // 2 + k, NY)
+
+    def y_lanes(k):
+        return pl.ds(pl.multiple_of(y_at(k) * 128, 128), 128)
+
+    def load(i):
+        lanes = y_lanes(ORDER[i])
+        return pltpu.make_async_copy(x_hbm.at[:, :, lanes], x_ref.at[:, :, lanes], lsem.at[i])
+
+    for i in range(NY):
+        load(i).start()
     def elem_peer(k):
         return lax.rem(em + k, NE)
 
@@ -78,6 +101,7 @@
     lax.fori_loop(1, NE, greet_elem, 0)
     lax.fori_loop(1, NP, greet_pulse, 0)
 
+    small[0].wait()
     keep = mask_ref[...].astype(F32)
     blocks_of = iota((BLOCKS, CELLS), 1) // (CELLS // BLOCKS) == iota((BLOCKS, CELLS), 0)
     keep_cells = jnp.dot(keep, jnp.where(blocks_of, 1.0, 0.0), preferred_element_type=F32)
@@ -99,51 +123,56 @@
 
     low_half = iota((32, 128), 1) < LC
 
-    def pack(step, carry):
-        pair = step // 8
-        c = (step // 4) % 2
-        group = step % 4
-        lanes = pl.ds(pl.multiple_of(pair * 256, 256), 256)
+    def pack(group, k):
+        lanes = y_lanes(k)
         rows = pl.ds(pl.multiple_of(group * 256, 256), 256)
-        turned = jnp.dot(perm[...], x_ref[c, rows, lanes], preferred_element_type=F32)
-        parts = [turned[32 * p : 32 * p + 32] for p in range(RUN)]
-        slots = []
-        for s in range(SLOTS):
-            total = parts[s] * coef[3 * s : 3 * s + 1, lanes]
-            for d in (1, 2):
-                total = total + parts[s + d] * coef[3 * s + d : 3 * s + d + 1, lanes]
-            slots.append(total)
-        for t in range(2):
+        both = jnp.concatenate([x_ref[0, rows, lanes], x_ref[1, rows, lanes]], axis=1)
+        turned = jnp.dot(perm[...], both, preferred_element_type=F32)
+        at = pl.ds(pl.multiple_of(group * 32, 32), 32)
+        for c in range(2):
+            parts = [turned[32 * p : 32 * p + 32, 128 * c : 128 * c + 128] for p in range(RUN)]
+            slots = []
+            for s in range(SLOTS):
+                total = parts[s] * coef[3 * s : 3 * s + 1, lanes]
+                for d in (1, 2):
+                    total = total + parts[s + d] * coef[3 * s + d : 3 * s + d + 1, lanes]
+                slots.append(total)
             for j in range(CHUNKS):
-                a = slots[j][:, 128 * t : 128 * t + 128]
-                b = slots[j + 3][:, 128 * t : 128 * t + 128]
+                a, b = slots[j], slots[j + 3]
                 first = jnp.where(low_half, a, pltpu.roll(b, LC, 1))
                 second = jnp.where(low_half, pltpu.roll(a, LC, 1), b)
-                at = pl.ds(pl.multiple_of(group * 32, 32), 32)
-                to = pl.ds(pl.multiple_of(c * 128, 128), 128)
-                prep[j, 4 * pair + 2 * t, at, to] = first.astype(BF16)
-                prep[j, 4 * pair + 2 * t + 1, at, to] = second.astype(BF16)
-        return carry
-
-    lax.fori_loop(0, 32, pack, 0)
-
-    pl.semaphore_wait(barrier, NE + NP - 2)
+                prep[j, 2 * y_at(k), at, 128 * c : 128 * c + 128] = first.astype(BF16)
+                prep[j, 2 * y_at(k) + 1, at, 128 * c : 128 * c + 128] = second.astype(BF16)
+        return k
 
     my_rows = pl.ds(pl.multiple_of(em * LE, LE), LE)
 
+    def samples(j, peer):
+        return pltpu.make_async_remote_copy(
+            src_ref=prep.at[j, peer],
+            dst_ref=xbuf.at[j, my_rows],
+            send_sem=xsend.at[j],
+            recv_sem=xrecv.at[j],
+            device_id=(peer, pm),
+            device_id_type=pl.DeviceIdType.MESH,
+        )
+
+    def send_y(j, k):
+        mate = 2 * y_at(k) + 1 - lax.rem(em, 2)
+        samples(j, mate).start()
+        if k:
+            samples(j, 2 * y_at(k) + lax.rem(em, 2)).start()
+
+    for i in range(NY):
+        load(i).wait()
+        lax.fori_loop(0, 4, pack, ORDER[i])
+        if i == 0:
+            pl.semaphore_wait(barrier, NE + NP - 2)
+        send_y(0, ORDER[i])
+
     def send_samples(j):
-        def one(k, carry):
-            pltpu.make_async_remote_copy(
-                src_ref=prep.at[j, elem_peer(k)],
-                dst_ref=xbuf.at[j, my_rows],
-                send_sem=xsend.at[j],
-                recv_sem=xrecv.at[j],
-                device_id=(elem_peer(k), pm),
-                device_id_type=pl.DeviceIdType.MESH,
-            ).start()
-            return carry
-
-        lax.fori_loop(1, NE, one, 0)
+        for k in ORDER:
+            send_y(j, k)
 
     def send_slots(k, carry):
         pltpu.make_async_remote_copy(
@@ -156,13 +185,14 @@
         ).start()
         return carry
 
-    send_samples(0)
+    send_samples(1)
     lax.fori_loop(1, NP, send_slots, 0)
-    send_samples(1)
     send_samples(2)
     for j in range(CHUNKS):
         xbuf[j, my_rows, :] = prep[j, em]
 
+    for copy in small[1:]:
+        copy.wait()
     eye = iota((128, 128), 0) == iota((128, 128), 1)
     for i in range(BEAMS // 128):
         line = index_ref[0:1, 128 * i : 128 * i + 128].astype(F32)
@@ -289,9 +319,15 @@
     power = pl.pallas_call(
         kernel,
         out_shape=jax.ShapeDtypeStruct((LB, LC, PULSES), F32),
-        in_specs=[vmem] * 6,
+        in_specs=[pl.BlockSpec(memory_space=pltpu.HBM)] * 6,
         out_specs=vmem,
         scratch_shapes=[
+            pltpu.VMEM((2, LE * RUN, CELLS), BF16),
+            pltpu.VMEM(keep_mask.shape, I32),
+            pltpu.VMEM((1, steer_index.shape[0]), I32),
+            pltpu.VMEM((1, element_position.shape[0]), F32),
+            pltpu.VMEM(element_gain.shape, F32),
+            pltpu.VMEM((1, steer_sines.shape[0]), F32),
             pltpu.VMEM((CHUNKS, NE, LE, 256), BF16),
             pltpu.VMEM((CHUNKS, E, 256), BF16),
             pltpu.VMEM((BEAMS, E), BF16),
@@ -307,10 +343,10 @@
             pltpu.VMEM((2, 2, 512, 512), BF16),
             pltpu.VMEM((2, 512, 512), BF16),
             pltpu.VMEM((BEAMS, 128), F32),
-            dma, dma, dma((CHUNKS,)), dma((CHUNKS,)), dma((CHUNKS,)), dma((CHUNKS,)),
+            dma((NY,)), dma((5,)), dma, dma, dma((CHUNKS,)), dma((CHUNKS,)), dma((CHUNKS,)), dma((CHUNKS,)),
         ],
         compiler_params=pltpu.CompilerParams(
-            collective_id=0, has_side_effects=True, vmem_limit_bytes=48 << 20
+            collective_id=0, has_side_effects=True, vmem_limit_bytes=63_000_000
         ),
         name="integrate",
     )(

time: 110 us -> 101 us (0.918); the launches traced: 109 us -> 101 us
  local copies, waits for them, and re-layouts: 6.63 us -> 2.29 us
  Pallas kernels: 102 us -> 98.9 us
    unnamed x13 -> x1, local copies, waits for them, and re-layouts: 6.63 us -> 2.29 us
    pallas_call x1, Pallas kernels: 102 us -> 98.9 us  [per_device(): pl.pallas_call(kernel, out_shape=jax.ShapeDtypeStruct((LB, LC, PULSES), F...]
where the time goes in v1:
time: 101 us
  Pallas kernels  98.9 us (98%)
  local copies, waits for them, and re-layouts  2.29 us (2%)
    pallas_call x1, Pallas kernels, per_device(): pl.pallas_call(kernel, out_shape=jax.ShapeDtypeStruct((LB, LC, PULSES), F...  98.9 us
    unnamed x1, local copies, waits for them, and re-layouts  2.29 us

profile of v1, /device:TPU:1, one launch (start us, length us, event | category | flops | bytes accessed | tf_op | source)
XLA Modules:
  0.0 101.2 jit_solution(14357708862458643936)
XLA Ops:
  0.0 98.9 %integrate.1 = f32[16,64,256]{2,1,0:T(8,128)} custom-call(bf16[2,1024,1024]{2,1,0:T(8,128)(2,1)} %bitcast.6, s32[8,32]{1,0:T(8,128)} %mask_hbm.1, s32[1,512]{1,0:T(1,128)} %bitcast.9, f32[1,2048]{1,0:T(1,128)} %bitcast.7, f32[2,2048]{1,0:T(2,128)} %gain_hbm.1, f32[1,1024]{1,0:T(1,128)} %bitcast.8), custom_call_target="tpu_custom_call" | custom-call | tf_op jit(solution)/shard_map/integrate/pallas_call | solution.py:319
  99.0 2.3 %copy.8 = f32[16,256,64]{1,2,0:T(8,128)} copy(f32[16,256,64]{1,2,0:T(8,128)} %bitcast.5) | data formatting | bytes 2097152

commit v2 on v1

--- a/solution.py
+++ b/solution.py
@@ -25,6 +25,9 @@
 LC = CELLS // NE
 CHUNKS = 3
 NY = 8
+UP, OWN, DOWN = 0, 7, 9
+TILES = 12
+HALF = BEAMS // 2
 ORDER = (3, 5, 4, 2, 6, 1, 7, 0)
 
 
@@ -56,8 +59,8 @@
 
 def kernel(
     x_hbm, mask_hbm, index_hbm, pos_hbm, gain_hbm, sines_hbm, out_ref,
-    x_ref, mask_ref, index_ref, pos_ref, gain_ref, sines_ref, prep, xbuf, wr, wi, beams, ybuf, fbuf, mine, mbuf, coef, perm, tab, tsel, xt, column,
-    lsem, ssem, msend, mrecv, xsend, xrecv, bsend, brecv,
+    x_ref, mask_ref, index_ref, pos_ref, gain_ref, sines_ref, prep, xbuf, wr, wi, psend, pbuf, own, beams, ybuf, fbuf, mine, mbuf, coef, perm, tab, tsel, xt, column,
+    lsem, ssem, msend, mrecv, xsend, xrecv, ssum, rsum, bsend, brecv,
 ):
     em = lax.axis_index("elem")
     pm = lax.axis_index("pulse")
@@ -145,34 +148,36 @@
                 prep[j, 2 * y_at(k) + 1, at, 128 * c : 128 * c + 128] = second.astype(BF16)
         return k
 
-    my_rows = pl.ds(pl.multiple_of(em * LE, LE), LE)
-
-    def samples(j, peer):
-        return pltpu.make_async_remote_copy(
-            src_ref=prep.at[j, peer],
-            dst_ref=xbuf.at[j, my_rows],
-            send_sem=xsend.at[j],
-            recv_sem=xrecv.at[j],
-            device_id=(peer, pm),
-            device_id_type=pl.DeviceIdType.MESH,
-        )
+    half = lax.rem(em, 2)
+
+    def place(k, mate):
+        if k == 0:
+            return 0, OWN + half
+        if k == 4:
+            return (5, DOWN + 6) if mate else (3, UP)
+        if k < 4:
+            return k - 1, UP + 7 - 2 * k + half
+        return (k + 1) % NY, DOWN + 2 * (7 - k) + half
+
+    def block_rows(block):
+        return pl.ds(pl.multiple_of(block * LE, LE), LE)
 
     def send_y(j, k):
-        mate = 2 * y_at(k) + 1 - lax.rem(em, 2)
-        samples(j, mate).start()
-        if k:
-            samples(j, 2 * y_at(k) + lax.rem(em, 2)).start()
-
-    for i in range(NY):
-        load(i).wait()
-        lax.fori_loop(0, 4, pack, ORDER[i])
-        if i == 0:
-            pl.semaphore_wait(barrier, NE + NP - 2)
-        send_y(0, ORDER[i])
-
-    def send_samples(j):
-        for k in ORDER:
-            send_y(j, k)
+        for mate in (1, 0):
+            k2, block = place(k, mate)
+            side = 1 - half if mate else half
+            source = prep.at[j, 2 * y_at(k) + side]
+            if k2 or mate:
+                pltpu.make_async_remote_copy(
+                    src_ref=source,
+                    dst_ref=xbuf.at[j, block_rows(block)],
+                    send_sem=xsend.at[j],
+                    recv_sem=xrecv.at[j],
+                    device_id=(2 * y_at(k2) + side, pm),
+                    device_id_type=pl.DeviceIdType.MESH,
+                ).start()
+            else:
+                xbuf[j, block_rows(block), :] = prep[j, 2 * y_at(k) + side]
 
     def send_slots(k, carry):
         pltpu.make_async_remote_copy(
@@ -185,18 +190,24 @@
         ).start()
         return carry
 
-    send_samples(1)
-    lax.fori_loop(1, NP, send_slots, 0)
-    send_samples(2)
-    for j in range(CHUNKS):
-        xbuf[j, my_rows, :] = prep[j, em]
+    for i in range(NY):
+        load(i).wait()
+        lax.fori_loop(0, 4, pack, ORDER[i])
+        if i == 0:
+            pl.semaphore_wait(barrier, NE + NP - 2)
+        send_y(0, ORDER[i])
+        if i == 0:
+            lax.fori_loop(1, NP, send_slots, 0)
+    for k in ORDER:
+        send_y(1, k)
 
     for copy in small[1:]:
         copy.wait()
-    eye = iota((128, 128), 0) == iota((128, 128), 1)
+    row, col = iota((128, 256), 0), iota((128, 256), 1)
     for i in range(BEAMS // 128):
-        line = index_ref[0:1, 128 * i : 128 * i + 128].astype(F32)
-        wanted = jnp.sum(jnp.where(eye, line, 0.0), axis=1, keepdims=True)
+        here = col == (row // LB) * (2 * LB) + LB * (i // 2) + row % LB
+        line = index_ref[0:1, 256 * (i % 2) : 256 * (i % 2) + 256].astype(F32)
+        wanted = jnp.sum(jnp.where(here, line, 0.0), axis=1, keepdims=True)
         choice = iota((128, sines_ref.shape[1]), 1).astype(F32) == wanted
         picked = jnp.sum(jnp.where(choice, sines_ref[...], 0.0), axis=1, keepdims=True)
         column[128 * i : 128 * i + 128, :] = jnp.broadcast_to(picked, (128, 128))
@@ -204,16 +215,21 @@
     factor = 1.0 / math.sqrt(E)
 
     def weigh(step, carry):
-        rows = pl.ds(pl.multiple_of((step // 16) * 64, 64), 64)
-        lanes = pl.ds(pl.multiple_of((step % 16) * 128, 128), 128)
+        rows = pl.ds(pl.multiple_of((step % 8) * 64, 64), 64)
+        tile = step // 8
+        to = pl.ds(pl.multiple_of(tile * 128, 128), 128)
+        middle = lax.rem(2 * y_at(0) + tile + 11, NE)
+        last = 2 * y_at(3) + 1 - half
+        source = jnp.where(tile == 0, 2 * y_at(5) + half, jnp.where(tile == TILES - 1, last, middle))
+        lanes = pl.ds(pl.multiple_of(source * 128, 128), 128)
         turns = pos_ref[0:1, lanes] * column[rows, :]
         cosine, sine = turn(turns - jnp.round(turns))
         real, imag = gain_ref[0:1, lanes] * factor, gain_ref[1:2, lanes] * factor
-        wr[rows, lanes] = (real * cosine + imag * sine).astype(BF16)
-        wi[rows, lanes] = (imag * cosine - real * sine).astype(BF16)
+        wr[rows, to] = (real * cosine + imag * sine).astype(BF16)
+        wi[rows, to] = (imag * cosine - real * sine).astype(BF16)
         return carry
 
-    lax.fori_loop(0, 8 * 16, weigh, 0)
+    lax.fori_loop(0, 8 * TILES, weigh, 0)
 
     def tabulate(step, carry):
         rows = pl.ds(pl.multiple_of(step * 32, 32), 32)
@@ -234,54 +250,102 @@
     def wait_bytes(ref, sem):
         pltpu.make_async_copy(ref, ref, sem).wait()
 
-    wait_bytes(mbuf.at[pl.ds(0, RUN * (NP - 1))], mrecv)
-    lane = iota((128, 128), 1)
-    for k in range(2):
-        for h in range(2):
-            found = [mbuf[pl.ds(j + 3 * h, NP, stride=RUN), :] for j in range(CHUNKS)]
-            found = jnp.concatenate(found + [jnp.zeros((NP, 128), F32)], axis=0)
-            pulse = jnp.sum(jnp.where(lane == 2 * em + k, found, 0.0), axis=1, keepdims=True)
-            row = iota((128, PULSES), 0)
-            target = (RUN * (row % NP)).astype(F32) + pulse
-            hit = (jnp.abs(iota((128, PULSES), 1).astype(F32) - target) < 0.5) & (row < 96)
-            rows = jnp.dot(jnp.where(hit, 1.0, 0.0).astype(BF16), tab[...], preferred_element_type=F32)
-            for part in range(2):
-                cosine = rows[:, 512 * part : 512 * part + 256]
-                sine = rows[:, 512 * part + 256 : 512 * part + 512]
-                real = slice(128 * h, 128 * h + 128)
-                imag = slice(256 + 128 * h, 256 + 128 * h + 128)
-                tsel[k, part, real, 0:256] = cosine.astype(BF16)
-                tsel[k, part, real, 256:512] = (-sine).astype(BF16)
-                tsel[k, part, imag, 0:256] = sine.astype(BF16)
-                tsel[k, part, imag, 256:512] = cosine.astype(BF16)
-
-    my_beams = pl.ds(pl.multiple_of(pm * LB, LB), LB)
-    for j in range(CHUNKS):
-        wait_bytes(xbuf.at[j, pl.ds(0, LE * (NE - 1))], xrecv.at[j])
-
-        def form(m, carry, j=j):
-            rows = pl.ds(pl.multiple_of(m * 256, 256), 256)
-            by_real = jnp.dot(wr[rows, :], xbuf[j], preferred_element_type=F32)
-            by_imag = jnp.dot(wi[rows, :], xbuf[j], preferred_element_type=F32)
-            beams[j, rows, 0:128] = (by_real[:, 0:128] - by_imag[:, 128:256]).astype(BF16)
-            beams[j, rows, 128:256] = (by_real[:, 128:256] + by_imag[:, 0:128]).astype(BF16)
-            return carry
-
-        lax.fori_loop(0, 2, form, 0)
-
-        def send_beams(k, carry, j=j):
-            pltpu.make_async_remote_copy(
-                src_ref=beams.at[j, pl.ds(pl.multiple_of(pulse_peer(k) * LB, LB), LB)],
-                dst_ref=ybuf.at[j, my_beams],
-                send_sem=bsend.at[j],
-                recv_sem=brecv.at[j],
-                device_id=(em, pulse_peer(k)),
-                device_id_type=pl.DeviceIdType.MESH,
-            ).start()
-            return carry
-
-        lax.fori_loop(1, NP, send_beams, 0)
-        ybuf[j, my_beams, :] = beams[j, my_beams, :]
+    def pick_tables():
+        wait_bytes(mbuf.at[pl.ds(0, RUN * (NP - 1))], mrecv)
+        lane = iota((128, 128), 1)
+        for k in range(2):
+            for h in range(2):
+                found = [mbuf[pl.ds(j + 3 * h, NP, stride=RUN), :] for j in range(CHUNKS)]
+                found = jnp.concatenate(found + [jnp.zeros((NP, 128), F32)], axis=0)
+                pulse = jnp.sum(jnp.where(lane == 2 * em + k, found, 0.0), axis=1, keepdims=True)
+                row = iota((128, PULSES), 0)
+                target = (RUN * (row % NP)).astype(F32) + pulse
+                hit = (jnp.abs(iota((128, PULSES), 1).astype(F32) - target) < 0.5) & (row < 96)
+                rows = jnp.dot(jnp.where(hit, 1.0, 0.0).astype(BF16), tab[...], preferred_element_type=F32)
+                for part in range(2):
+                    cosine = rows[:, 512 * part : 512 * part + 256]
+                    sine = rows[:, 512 * part + 256 : 512 * part + 512]
+                    real = slice(128 * h, 128 * h + 128)
+                    imag = slice(256 + 128 * h, 256 + 128 * h + 128)
+                    tsel[k, part, real, 0:256] = cosine.astype(BF16)
+                    tsel[k, part, real, 256:512] = (-sine).astype(BF16)
+                    tsel[k, part, imag, 0:256] = sine.astype(BF16)
+                    tsel[k, part, imag, 256:512] = cosine.astype(BF16)
+
+    def product(rows, tile, block, count, j):
+        weights = pl.ds(128 * tile, 128 * count)
+        samples = xbuf[j, 128 * block : 128 * block + 128 * count, :]
+        by_real = jnp.dot(wr[rows, weights], samples, preferred_element_type=F32)
+        by_imag = jnp.dot(wi[rows, weights], samples, preferred_element_type=F32)
+        real = by_real[:, 0:128] - by_imag[:, 128:256]
+        return jnp.concatenate([real, by_real[:, 128:256] + by_imag[:, 0:128]], axis=1)
+
+    def sum_for_neighbours(j):
+        wait_bytes(xbuf.at[j, pl.ds(0, LE * 13)], xrecv.at[j])
+        for m in range(2):
+            rows = pl.ds(HALF * m, HALF)
+            for way, tile, block, k in ((0, 0, UP, 1), (1, 5, DOWN, 7)):
+                psend[j, way, rows, :] = product(rows, tile, block, 7, j).astype(BF16)
+                pltpu.make_async_remote_copy(
+                    src_ref=psend.at[j, way, rows],
+                    dst_ref=pbuf.at[j, way, rows],
+                    send_sem=ssum.at[j],
+                    recv_sem=rsum.at[2 * j + m],
+                    device_id=(2 * y_at(k) + half, pm),
+                    device_id_type=pl.DeviceIdType.MESH,
+                ).start()
+
+    def sum_own(j):
+        for m in range(2):
+            rows = pl.ds(HALF * m, HALF)
+            own[j, rows, :] = product(rows, 5, OWN, 2, j)
+
+    core = lax.rem(pm, 2)
+    my_beams = pl.ds(pl.multiple_of((core * (NP // 2) + pm // 2) * LB, LB), LB)
+    my_place = pl.ds(pl.multiple_of(pm * LB, LB), LB)
+
+    def beams_copy(j, m, k):
+        chip = lax.rem(pm // 2 + k, NP // 2)
+        return pltpu.make_async_remote_copy(
+            src_ref=beams.at[j, pl.ds(pl.multiple_of((m * (NP // 2) + chip) * LB, LB), LB)],
+            dst_ref=ybuf.at[j, my_place],
+            send_sem=bsend.at[j],
+            recv_sem=brecv.at[j],
+            device_id=(em, 2 * chip + m),
+            device_id_type=pl.DeviceIdType.MESH,
+        )
+
+    def finish_beams(j):
+        for m in range(2):
+            rows = pl.ds(HALF * m, HALF)
+            wait_bytes(pbuf.at[j, :, rows], rsum.at[2 * j + m])
+            total = own[j, rows, :] + pbuf[j, 0, rows, :].astype(F32) + pbuf[j, 1, rows, :].astype(F32)
+            beams[j, rows, :] = total.astype(BF16)
+
+            def one(k, carry, m=m):
+                beams_copy(j, m, lax.rem(5 * k, NP // 2)).start()
+                return carry
+
+            lax.fori_loop(1, NP // 2, one, 0)
+
+            @pl.when(core != m)
+            def _(m=m):
+                beams_copy(j, m, 0).start()
+
+        ybuf[j, my_place, :] = beams[j, my_beams, :]
+
+    sum_for_neighbours(0)
+    for k in ORDER:
+        send_y(2, k)
+    sum_own(0)
+    sum_for_neighbours(1)
+    pick_tables()
+    finish_beams(0)
+    sum_own(1)
+    sum_for_neighbours(2)
+    finish_beams(1)
+    sum_own(2)
+    finish_beams(2)
 
     for j in range(CHUNKS):
         wait_bytes(ybuf.at[j, pl.ds(0, LB * (NP - 1))], brecv.at[j])
@@ -309,7 +373,8 @@
 
     wait_bytes(mbuf.at[pl.ds(0, RUN * (NP - 1))], msend)
     for j in range(CHUNKS):
-        wait_bytes(xbuf.at[j, pl.ds(0, LE * (NE - 1))], xsend.at[j])
+        wait_bytes(xbuf.at[j, pl.ds(0, LE * 13)], xsend.at[j])
+        wait_bytes(psend.at[j], ssum.at[j])
         wait_bytes(ybuf.at[j, pl.ds(0, LB * (NP - 1))], bsend.at[j])
 
 
@@ -330,8 +395,11 @@
             pltpu.VMEM((1, steer_sines.shape[0]), F32),
             pltpu.VMEM((CHUNKS, NE, LE, 256), BF16),
             pltpu.VMEM((CHUNKS, E, 256), BF16),
-            pltpu.VMEM((BEAMS, E), BF16),
-            pltpu.VMEM((BEAMS, E), BF16),
+            pltpu.VMEM((BEAMS, 128 * TILES), BF16),
+            pltpu.VMEM((BEAMS, 128 * TILES), BF16),
+            pltpu.VMEM((CHUNKS, 2, BEAMS, 256), BF16),
+            pltpu.VMEM((CHUNKS, 2, BEAMS, 256), BF16),
+            pltpu.VMEM((CHUNKS, BEAMS, 256), F32),
             pltpu.VMEM((CHUNKS, BEAMS, 256), BF16),
             pltpu.VMEM((CHUNKS, BEAMS, 256), BF16),
             pltpu.VMEM((2, CHUNKS * BEAMS, 128), F32),
@@ -343,7 +411,7 @@
             pltpu.VMEM((2, 2, 512, 512), BF16),
             pltpu.VMEM((2, 512, 512), BF16),
             pltpu.VMEM((BEAMS, 128), F32),
-            dma((NY,)), dma((5,)), dma, dma, dma((CHUNKS,)), dma((CHUNKS,)), dma((CHUNKS,)), dma((CHUNKS,)),
+            dma((NY,)), dma((5,)), dma, dma, dma((CHUNKS,)), dma((CHUNKS,)), dma((CHUNKS,)), dma((2 * CHUNKS,)), dma((CHUNKS,)), dma((CHUNKS,)),
         ],
         compiler_params=pltpu.CompilerParams(
             collective_id=0, has_side_effects=True, vmem_limit_bytes=63_000_000

time: 101 us -> 85.5 us (0.85)
  Pallas kernels: 98.9 us -> 83.1 us
    pallas_call x1, Pallas kernels: 98.9 us -> 83.1 us  [per_device(): pl.pallas_call(kernel, out_shape=jax.ShapeDtypeStruct((LB, LC, PULSES), F...]
where the time goes in v2:
time: 85.5 us; the launch traced here: 85.4 us
  Pallas kernels  83.1 us (97%)
  local copies, waits for them, and re-layouts  2.29 us (3%)
    pallas_call x1, Pallas kernels, per_device(): pl.pallas_call(kernel, out_shape=jax.ShapeDtypeStruct((LB, LC, PULSES), F...  83.1 us
    unnamed x1, local copies, waits for them, and re-layouts  2.29 us

profile of v2, /device:TPU:1, one launch (start us, length us, event | category | flops | bytes accessed | tf_op | source)
XLA Modules:
  0.0 85.4 jit_solution(16788755179706477365)
XLA Ops:
  0.0 83.1 %integrate.1 = f32[16,64,256]{2,1,0:T(8,128)} custom-call(bf16[2,1024,1024]{2,1,0:T(8,128)(2,1)} %bitcast.6, s32[8,32]{1,0:T(8,128)} %mask_hbm.1, s32[1,512]{1,0:T(1,128)} %bitcast.9, f32[1,2048]{1,0:T(1,128)} %bitcast.7, f32[2,2048]{1,0:T(2,128)} %gain_hbm.1, f32[1,1024]{1,0:T(1,128)} %bitcast.8), custom_call_target="tpu_custom_call" | custom-call | tf_op jit(solution)/shard_map/integrate/pallas_call | solution.py:384
  83.1 2.3 %copy.8 = f32[16,256,64]{1,2,0:T(8,128)} copy(f32[16,256,64]{1,2,0:T(8,128)} %bitcast.5) | data formatting | bytes 2097152

commit v3 on v2

--- a/solution.py
+++ b/solution.py
@@ -23,7 +23,8 @@
 LE = E // NE
 LB = BEAMS // NP
 LC = CELLS // NE
-CHUNKS = 3
+CHUNKS = SLOTS
+AHEAD = 3
 NY = 8
 UP, OWN, DOWN = 0, 7, 9
 TILES = 12
@@ -132,6 +133,7 @@
         both = jnp.concatenate([x_ref[0, rows, lanes], x_ref[1, rows, lanes]], axis=1)
         turned = jnp.dot(perm[...], both, preferred_element_type=F32)
         at = pl.ds(pl.multiple_of(group * 32, 32), 32)
+        packed = []
         for c in range(2):
             parts = [turned[32 * p : 32 * p + 32, 128 * c : 128 * c + 128] for p in range(RUN)]
             slots = []
@@ -140,12 +142,13 @@
                 for d in (1, 2):
                     total = total + parts[s + d] * coef[3 * s + d : 3 * s + d + 1, lanes]
                 slots.append(total)
-            for j in range(CHUNKS):
-                a, b = slots[j], slots[j + 3]
-                first = jnp.where(low_half, a, pltpu.roll(b, LC, 1))
-                second = jnp.where(low_half, pltpu.roll(a, LC, 1), b)
-                prep[j, 2 * y_at(k), at, 128 * c : 128 * c + 128] = first.astype(BF16)
-                prep[j, 2 * y_at(k) + 1, at, 128 * c : 128 * c + 128] = second.astype(BF16)
+            packed.append(slots)
+        for j in range(CHUNKS):
+            a, b = packed[0][j], packed[1][j]
+            first = jnp.where(low_half, a, pltpu.roll(b, LC, 1))
+            second = jnp.where(low_half, pltpu.roll(a, LC, 1), b)
+            prep[j, 2 * y_at(k), at, :] = first.astype(BF16)
+            prep[j, 2 * y_at(k) + 1, at, :] = second.astype(BF16)
         return k
 
     half = lax.rem(em, 2)
@@ -198,8 +201,13 @@
         send_y(0, ORDER[i])
         if i == 0:
             lax.fori_loop(1, NP, send_slots, 0)
-    for k in ORDER:
-        send_y(1, k)
+
+    def send_chunk(j, carry):
+        for k in ORDER:
+            send_y(j, k)
+        return carry
+
+    lax.fori_loop(1, AHEAD, send_chunk, 0)
 
     for copy in small[1:]:
         copy.wait()
@@ -255,7 +263,7 @@
         lane = iota((128, 128), 1)
         for k in range(2):
             for h in range(2):
-                found = [mbuf[pl.ds(j + 3 * h, NP, stride=RUN), :] for j in range(CHUNKS)]
+                found = [mbuf[pl.ds(j + 3 * h, NP, stride=RUN), :] for j in range(3)]
                 found = jnp.concatenate(found + [jnp.zeros((NP, 128), F32)], axis=0)
                 pulse = jnp.sum(jnp.where(lane == 2 * em + k, found, 0.0), axis=1, keepdims=True)
                 row = iota((128, PULSES), 0)
@@ -277,8 +285,8 @@
         samples = xbuf[j, 128 * block : 128 * block + 128 * count, :]
         by_real = jnp.dot(wr[rows, weights], samples, preferred_element_type=F32)
         by_imag = jnp.dot(wi[rows, weights], samples, preferred_element_type=F32)
-        real = by_real[:, 0:128] - by_imag[:, 128:256]
-        return jnp.concatenate([real, by_real[:, 128:256] + by_imag[:, 0:128]], axis=1)
+        crossed = pltpu.roll(by_imag, LC, 1)
+        return by_real + jnp.where(iota(crossed.shape, 1) < LC, -crossed, crossed)
 
     def sum_for_neighbours(j):
         wait_bytes(xbuf.at[j, pl.ds(0, LE * 13)], xrecv.at[j])
@@ -334,33 +342,38 @@
 
         ybuf[j, my_place, :] = beams[j, my_beams, :]
 
-    sum_for_neighbours(0)
-    for k in ORDER:
-        send_y(2, k)
-    sum_own(0)
-    sum_for_neighbours(1)
     pick_tables()
-    finish_beams(0)
-    sum_own(1)
-    sum_for_neighbours(2)
-    finish_beams(1)
-    sum_own(2)
-    finish_beams(2)
-
-    for j in range(CHUNKS):
-        wait_bytes(ybuf.at[j, pl.ds(0, LB * (NP - 1))], brecv.at[j])
-        fbuf[0, 512 * j : 512 * j + 512, :] = ybuf[j, :, 0:128].astype(F32)
-        fbuf[1, 512 * j : 512 * j + 512, :] = ybuf[j, :, 128:256].astype(F32)
-
-    for b in range(LB):
-        for c in range(2):
-            got = [fbuf[c, pl.ds(512 * j + b, NP, stride=LB), :] for j in range(CHUNKS)]
+
+    def advance(j, carry):
+        sum_for_neighbours(j)
+
+        @pl.when(j < CHUNKS - AHEAD)
+        def _():
+            send_chunk(j + AHEAD, 0)
+
+        @pl.when(j > 1)
+        def _():
+            finish_beams(j - 2)
+
+        sum_own(j)
+        return carry
+
+    lax.fori_loop(0, CHUNKS, advance, 0)
+    finish_beams(CHUNKS - 2)
+    finish_beams(CHUNKS - 1)
+
+    for h in range(2):
+        for j in range(3 * h, 3 * h + 3):
+            wait_bytes(ybuf.at[j, pl.ds(0, LB * (NP - 1))], brecv.at[j])
+            fbuf[512 * j : 512 * j + 512, :] = ybuf[j].astype(F32)
+        for b in range(LB):
+            got = [fbuf[pl.ds(512 * (3 * h + j) + b, NP, stride=LB), :] for j in range(3)]
             got = jnp.concatenate(got + [jnp.zeros((NP, 128), F32)], axis=0)
             flat = got.T.astype(BF16)
-            for h in range(2):
+            for c in range(2):
                 for k in range(2):
                     xt[k, 32 * b : 32 * b + 32, 256 * c + 128 * h : 256 * c + 128 * h + 128] = flat[
-                        64 * h + 32 * k : 64 * h + 32 * k + 32
+                        64 * c + 32 * k : 64 * c + 32 * k + 32
                     ]
 
     for k in range(2):
@@ -393,16 +406,16 @@
             pltpu.VMEM((1, element_position.shape[0]), F32),
             pltpu.VMEM(element_gain.shape, F32),
             pltpu.VMEM((1, steer_sines.shape[0]), F32),
-            pltpu.VMEM((CHUNKS, NE, LE, 256), BF16),
-            pltpu.VMEM((CHUNKS, E, 256), BF16),
+            pltpu.VMEM((CHUNKS, NE, LE, 128), BF16),
+            pltpu.VMEM((CHUNKS, E, 128), BF16),
             pltpu.VMEM((BEAMS, 128 * TILES), BF16),
             pltpu.VMEM((BEAMS, 128 * TILES), BF16),
-            pltpu.VMEM((CHUNKS, 2, BEAMS, 256), BF16),
-            pltpu.VMEM((CHUNKS, 2, BEAMS, 256), BF16),
-            pltpu.VMEM((CHUNKS, BEAMS, 256), F32),
-            pltpu.VMEM((CHUNKS, BEAMS, 256), BF16),
-            pltpu.VMEM((CHUNKS, BEAMS, 256), BF16),
-            pltpu.VMEM((2, CHUNKS * BEAMS, 128), F32),
+            pltpu.VMEM((CHUNKS, 2, BEAMS, 128), BF16),
+            pltpu.VMEM((CHUNKS, 2, BEAMS, 128), BF16),
+            pltpu.VMEM((CHUNKS, BEAMS, 128), F32),
+            pltpu.VMEM((CHUNKS, BEAMS, 128), BF16),
+            pltpu.VMEM((CHUNKS, BEAMS, 128), BF16),
+            pltpu.VMEM((CHUNKS * BEAMS, 128), F32),
             pltpu.VMEM((RUN, 128), F32),
             pltpu.VMEM((RUN * NP, 128), F32),
             pltpu.VMEM((3 * SLOTS, CELLS), F32),
@@ -414,16 +427,21 @@
             dma((NY,)), dma((5,)), dma, dma, dma((CHUNKS,)), dma((CHUNKS,)), dma((CHUNKS,)), dma((2 * CHUNKS,)), dma((CHUNKS,)), dma((CHUNKS,)),
         ],
         compiler_params=pltpu.CompilerParams(
-            collective_id=0, has_side_effects=True, vmem_limit_bytes=63_000_000
+            collective_id=0, has_side_effects=True, vmem_limit_bytes=40 << 20
         ),
         name="integrate",
     )(
-        echoes.reshape(2, LE * RUN, CELLS),
-        keep_mask,
-        steer_index.reshape(1, -1),
-        element_position.reshape(1, -1),
-        element_gain,
-        steer_sines.reshape(1, -1),
+        *(
+            pltpu.with_memory_space_constraint(value, pltpu.HBM)
+            for value in (
+                echoes.reshape(2, LE * RUN, CELLS),
+                keep_mask,
+                steer_index.reshape(1, -1),
+                element_position.reshape(1, -1),
+                element_gain,
+                steer_sines.reshape(1, -1),
+            )
+        )
     )
     return jnp.transpose(power, (0, 2, 1))
 

time: 85.5 us -> 82.7 us (0.967)
  Pallas kernels: 83.1 us -> 81.6 us
  local copies, waits for them, and re-layouts: 2.29 us -> 0.97 us
    pallas_call x1, Pallas kernels: 83.1 us -> 81.6 us  [per_device(): pl.pallas_call(kernel, out_shape=jax.ShapeDtypeStruct((LB, LC, PULSES), F...]
    unnamed x1, local copies, waits for them, and re-layouts: 2.29 us -> 0.97 us
where the time goes in v3:
time: 82.7 us; the launch traced here: 82.6 us
  Pallas kernels  81.6 us (99%)
  local copies, waits for them, and re-layouts  0.97 us (1%)
    pallas_call x1, Pallas kernels, per_device(): pl.pallas_call(kernel, out_shape=jax.ShapeDtypeStruct((LB, LC, PULSES), F...  81.6 us

profile of v3, /device:TPU:1, one launch (start us, length us, event | category | flops | bytes accessed | tf_op | source)
XLA Modules:
  0.0 82.6 jit_solution(18109994010214238399)
XLA Ops:
  0.0 81.6 %integrate.1 = f32[16,64,256]{2,1,0:T(8,128)S(1)} custom-call(bf16[2,1024,1024]{2,1,0:T(8,128)(2,1)} %bitcast.6, s32[8,32]{1,0:T(8,128)} %mask_hbm.1, s32[1,512]{1,0:T(1,128)} %bitcast.9, f32[1,2048]{1,0:T(1,128)} %bitcast.7, f32[2,2048]{1,0:T(2,128)} %gain_hbm.1, f32[1,1024]{1,0:T(1,128)} %bitcast.8), custom_call_target="tpu_custom_call" | custom-call | tf_op jit(solution)/shard_map/integrate/pallas_call | solution.py:397
  81.6 1.0 %copy.8 = f32[16,256,64]{1,2,0:T(8,128)} copy(f32[16,256,64]{1,2,0:T(8,128)S(1)} %bitcast.5) | data formatting | bytes 2097152
